TPU v7x, 256 devices: a whole 4x4x8 slice. The times are simulated.
256 devices in a mesh: section: 4 (over z_hi), dp: 64 (over y, x, z_lo, core).
Axes of the slice: x: 4, y: 4, z: 8 (z_hi: 4, z_lo: 2; z = z_hi * 2 + z_lo), core: 2. Of those that a mesh axis runs over, the one named last changes fastest.
Arguments:
- activations: bfloat16 [4, 2, 4096, 2048], P('section', None, 'dp'), may hold values from -6 to 6
- routes: int32 [4, 2, 4096, 8], P('section', None, 'dp'), may hold values from 0 to 63, all different within a row; in each aligned block of 64 rows (0 to 63, 64 to 127, ..., all dimensions but the last counted through in order) at most 12 rows name the same one
- gates: bfloat16 [4, 2, 4096, 8], P('section', None, 'dp'), may hold values from 0.099609375 to 1
- hidden_cot: bfloat16 [4, 2, 64, 768, 768], P('section', None, 'dp'), may hold values from -1 to 1
- weight: bfloat16 [4, 64, 2048, 768], P('section', 'dp'), may hold values from -0.21875 to 0.21875
- top_cot: bfloat16 [2, 4096, 2048], P(None, 'dp'), may hold values from -1.1953125 to 1.1953125
Outputs:
- grad_sum: bfloat16 [4, 64, 2048, 768], P('section', 'dp')
- fisher: bfloat16 [4, 64, 2048, 768], P('section', 'dp')
- resid_grad: bfloat16 [4, 2, 4096, 2048], P('section', None, 'dp')
Inputs may be any that keep to these rules, and one draw needn't show every extreme that they name: `routes`: each token names 8 different experts; among the tokens of one block of 64 of one section and micro-batch no expert is named by more than 12 tokens, a bound that some block reaches.
All inputs are finite; a program needn't handle non-finite values.
Results may differ from a plain program's by a relative error of at most 0.0054.
Values may be sent and summed in bfloat16 or wider, within the bound.
A program may use at most 128 MiB of HBM per device.

v0:
```python
from functools import partial

import jax
import jax.numpy as jnp
from jax import lax
from jax.sharding import PartitionSpec as P


def prefix(value, axis, join, neutral):
    count, mine = (lax.axis_size(axis), lax.axis_index(axis))
    pieces = lax.all_gather(value, axis)
    pieces = pieces[::-1]
    mine = count - 1 - mine
    so_far = jnp.full_like(value, 0) + jnp.asarray(neutral, value.dtype)

    def lap(position, so_far):
        longer = join(so_far, pieces[position])
        return jnp.where(position < mine, longer, so_far)

    return lax.fori_loop(0, count - 1, lap, so_far)


def slot_positions(block_routes, count):
    flat_ids = block_routes.reshape(-1)
    onehot = (flat_ids[:, None] == jnp.arange(count, dtype=jnp.int32)[None, :]).astype(jnp.int32)
    earlier = jnp.cumsum(onehot, axis=0) - onehot
    return (flat_ids, jnp.sum(earlier * onehot, axis=1))


def dispatch_tables(block_routes, block_gates, experts, capacity):
    flat_ids, position = slot_positions(block_routes, experts)
    slot_ids = flat_ids * capacity + position
    matches = (
        slot_ids[:, None] == jnp.arange(experts * capacity, dtype=jnp.int32)[None, :]
    ).astype(jnp.float32)
    slot_gates = jnp.dot(block_gates.reshape(-1).astype(jnp.float32), matches)
    tok_count = block_routes.shape[0]
    dispatch_mat = (
        matches.reshape(tok_count, block_routes.shape[1], -1).sum(axis=1).astype(jnp.bfloat16)
    )
    return (dispatch_mat, slot_gates.astype(jnp.bfloat16))


def owner_work(received_rows, received_gates, cot_rows, expert_weight):
    scaled = (received_gates.astype(jnp.float32)[..., None] * cot_rows.astype(jnp.float32)).astype(
        jnp.bfloat16
    )
    partial_grad = jnp.einsum(
        "msd,msf->mdf", received_rows, scaled, preferred_element_type=jnp.float32
    )
    back_rows = jnp.einsum(
        "msf,df->msd", scaled, expert_weight, preferred_element_type=jnp.float32
    ).astype(jnp.bfloat16)
    return (partial_grad, back_rows)


def add_terms(earlier, later):
    return earlier + later


def shards(activations, routes, gates, hidden_cot, weight, top_cot):
    features = activations[0]
    route_ids = routes[0]
    gate_vals = gates[0]
    cotangent = hidden_cot[0, :, 0]
    expert_weight = weight[0, 0]
    experts = lax.axis_size("dp")
    slot_count = cotangent.shape[1]
    capacity = slot_count // experts
    batch_count = features.shape[0]
    model_width = features.shape[2]
    builder = partial(dispatch_tables, experts=experts, capacity=capacity)
    dispatch_mat, slot_gates = jax.vmap(builder)(route_ids, gate_vals)
    outgoing = jnp.einsum(
        "mtj,mtd->mjd", dispatch_mat, features, preferred_element_type=jnp.float32
    ).astype(jnp.bfloat16)
    outgoing = outgoing.reshape(batch_count, experts, capacity, model_width)
    outgoing_gates = slot_gates.reshape(batch_count, experts, capacity)
    rows_in, gates_in = (
        lax.all_to_all(outgoing, "dp", split_axis=1, concat_axis=2, tiled=True),
        lax.all_to_all(outgoing_gates, "dp", split_axis=1, concat_axis=2, tiled=True),
    )
    partial_grad, back_rows = owner_work(rows_in[:, 0], gates_in[:, 0], cotangent, expert_weight)
    returned = lax.all_to_all(back_rows[:, None], "dp", split_axis=2, concat_axis=1, tiled=True)
    combined = jnp.einsum(
        "mtj,mjd->mtd",
        dispatch_mat,
        returned.reshape(batch_count, experts * capacity, model_width),
        preferred_element_type=jnp.float32,
    )
    later = prefix(combined, "section", add_terms, jnp.zeros_like(combined))
    resid = (top_cot.astype(jnp.float32) + combined + later).astype(jnp.bfloat16)
    grad_total = jnp.sum(partial_grad, axis=0)
    fisher_total = jnp.sum(partial_grad * partial_grad, axis=0)
    return (
        grad_total[None, None].astype(jnp.bfloat16),
        fisher_total[None, None].astype(jnp.bfloat16),
        resid[None],
    )


def solution(mesh):
    return jax.shard_map(
        shards,
        mesh=mesh,
        in_specs=(
            P("section", None, "dp", None),
            P("section", None, "dp", None),
            P("section", None, "dp", None),
            P("section", None, "dp", None, None),
            P("section", "dp", None, None),
            P(None, "dp", None),
        ),
        out_specs=(
            P("section", "dp", None, None),
            P("section", "dp", None, None),
            P("section", None, "dp", None),
        ),
        check_vma=False,
    )
```

profile of v0, /device:TPU:6, one launch (start us, length us, event | category | flops | bytes accessed | tf_op | source)
XLA Modules:
  0.0 333.3 jit_solution(3922631504452818000)
XLA Ops:
  7.2 0.9 copy.40
  8.1 0.1 eq.49
  8.2 0.1 eq.45
  8.3 0.7 fusion.21
  9.0 4.5 %reduce-window.6 = s32[2,64,4,128]{3,1,2,0:T(8,128)S(1)} reduce-window(s32[2,64,4,128]{3,1,2,0:T(8,128)} %fusion.21, s32[]{:T(128)} %constant.36.clone.1), window={size=1x1x1x128 pad=0_0x0_0x0_0x127_0}, to_apply=%region_0.0 | reduce-window | flops 8323072 | bytes 524292 | tf_op jit(solution)/shard_map/reduce-window
  13.5 0.3 slice_reduce_fusion
  13.9 0.2 fusion.20
  14.1 0.8 copy.45
  14.9 0.1 reshape.93
  15.0 0.7 fusion.9
  15.7 0.1 reshape.84
  15.9 15.5 %all_to_all.12 = bf16[2,64,12]{2,0,1:T(2,128)(2,1)S(1)} all-to-all(bf16[2,64,12]{2,0,1:T(2,128)(2,1)S(1)} %copy.46), channel_id=1, replica_groups=mesh['section'=4,'dp'=64] {'dp'}, dimensions={1} | all-to-all | bytes 6144 | tf_op jit(solution)/shard_map/all_to_all | solution.py:81
  31.3 0.1 copy.47
  31.4 0.1 copy.48
  31.6 0.1 reshape.86
  31.7 7.0 %convert_bitcast_fusion = bf16[2,1,768,2048]{3,2,0,1:T(8,128)(2,1)S(1)} fusion(bf16[1,1,2048,768]{3,2,1,0:T(8,128)(2,1)S(1)} %copy-done, bf16[1,2,1,768,768]{4,3,2,1,0:T(8,128)(2,1)} %param.11, f32[2,768]{1,0:T(2,128)S(1)} %reshape.86), kind=kOutput, calls=%fused_computation.7 | convolution fusion | flops 4838522880 | bytes 11802624 | tf_op jit(solution)/shard_map/msf,df->msd/dot_general | solution.py:51
  38.7 18.8 %copy.50 = bf16[2,1,768,2048]{3,0,1,2:T(2,128)(2,1)} copy(bf16[2,1,768,2048]{3,2,0,1:T(8,128)(2,1)S(1)} %convert_bitcast_fusion) | data formatting | bytes 12582912 | tf_op jit(solution)/shard_map/broadcast_in_dim | solution.py:84
  57.5 7.3 %all-to-all-start.2 = ((bf16[2,1,768,2048]{3,0,1,2:T(2,128)(2,1)}), bf16[2,1,768,2048]{3,0,1,2:T(2,128)(2,1)}, u32[]{:S(2)}, u32[]{:S(2)}) async-start(bf16[2,1,768,2048]{3,0,1,2:T(2,128)(2,1)} %copy.50), calls=%async_computation.2 | async-start | bytes 12582912 | tf_op jit(solution)/shard_map/all_to_all | solution.py:84
  64.9 1.0 convert_reduce_fusion
  65.9 2.9 convolution_convert_fusion
  68.8 18.8 %copy.44 = bf16[2,768,2048]{2,0,1:T(2,128)(2,1)} copy(bf16[2,768,2048]{2,1,0:T(8,128)(2,1)S(1)} %convolution_convert_fusion) | data formatting | bytes 12582912 | tf_op jit(solution)/shard_map/convert_element_type | solution.py:76
  87.6 52.0 %all-to-all-done.2 = bf16[2,1,768,2048]{3,0,1,2:T(2,128)(2,1)} async-done(((bf16[2,1,768,2048]{3,0,1,2:T(2,128)(2,1)}), bf16[2,1,768,2048]{3,0,1,2:T(2,128)(2,1)}, u32[]{:S(2)}, u32[]{:S(2)}) %all-to-all-start.2) | async-done | bytes 6291488 | tf_op jit(solution)/shard_map/all_to_all | solution.py:84
  139.6 20.4 %all-to-all-start = ((bf16[2,64,12,2048]{3,0,2,1:T(2,128)(2,1)}), bf16[2,64,12,2048]{3,0,2,1:T(2,128)(2,1)}, u32[]{:S(2)}, u32[]{:S(2)}) async-start(bf16[2,64,12,2048]{3,0,2,1:T(2,128)(2,1)} %bitcast.73), calls=%async_computation | async-start | bytes 12582912 | tf_op jit(solution)/shard_map/all_to_all | solution.py:80
  160.0 7.4 %fusion = f32[2,64,2048]{2,1,0:T(8,128)} fusion(bf16[2,1,768,2048]{3,0,1,2:T(2,128)(2,1)} %all-to-all-done.2, bf16[2,64,768]{2,1,0:T(8,128)(2,1)S(1)} %convert_reduce_fusion), kind=kOutput, calls=%fused_computation.2 | convolution fusion | flops 402653184 | bytes 7536640 | tf_op jit(solution)/shard_map/mtj,mjd->mtd/dot_general | solution.py:85
  167.5 130.6 %all-to-all-done = bf16[2,64,12,2048]{3,0,2,1:T(2,128)(2,1)} async-done(((bf16[2,64,12,2048]{3,0,2,1:T(2,128)(2,1)}), bf16[2,64,12,2048]{3,0,2,1:T(2,128)(2,1)}, u32[]{:S(2)}, u32[]{:S(2)}) %all-to-all-start) | async-done | bytes 6291488 | tf_op jit(solution)/shard_map/all_to_all | solution.py:80
  298.1 13.3 %multiply_reduce_fusion = (bf16[2048,768]{1,0:T(8,128)(2,1)}, bf16[2048,768]{1,0:T(8,128)(2,1)}) fusion(bf16[1,2,1,768,768]{4,3,2,1,0:T(8,128)(2,1)} %param.11, f32[2,768]{1,0:T(2,128)S(1)} %reshape.86, bf16[2,768,2048]{2,0,1:T(2,128)(2,1)} %bitcast.4), kind=kOutput, calls=%fused_computation.1 | convolution fusion | flops 4841668608 | bytes 14948352 | tf_op jit(solution)/shard_map/msd,msf->mdf/dot_general | solution.py:48
  311.4 4.6 %rev.3 = f32[4,2,64,2048]{3,2,1,0:T(8,128)} reverse(f32[4,2,64,2048]{3,2,1,0:T(8,128)} %bitcast.74), dimensions={0} | reverse | bytes 8388608 | tf_op jit(solution)/shard_map/rev | solution.py:12
  316.0 7.7 %while.14 = (s32[]{:T(128)}, f32[2,64,2048]{2,1,0:T(8,128)}, s32[]{:T(128)}, f32[4,2,64,2048]{3,2,1,0:T(8,128)}, s32[]{:T(128)}, /*index=5*/s32[]{:T(128)}) while((s32[]{:T(128)}, f32[2,64,2048]{2,1,0:T(8,128)}, s32[]{:T(128)}, f32[4,2,64,2048]{3,2,1,0:T(8,128)}, s32[]{:T(128)}, /*index=5*/s32[]{:T(128)}) %tuple.37), condition=%wide.region_7.8_spmd.clone, body=%wide.region_6.7_spmd.clone.sunk | while | flops 786436 | bytes 3145821 | solution.py:20
  316.0 2.4 add_select_fusion.2
  318.4 2.7 add_select_fusion.2
  321.1 2.7 add_select_fusion.2
  323.8 2.6 fusion.16
  (13 shorter events, 0.3 us)
Async XLA Ops:
  7.2 24.5 %copy-start = (bf16[1,1,2048,768]{3,2,1,0:T(8,128)(2,1)S(1)}, bf16[1,1,2048,768]{3,2,1,0:T(8,128)(2,1)}, u32[]{:S(2)}) copy-start(bf16[1,1,2048,768]{3,2,1,0:T(8,128)(2,1)} %param.12) | copy-start | bytes 9437188
  57.5 82.1 %all-to-all-start.2 = ((bf16[2,1,768,2048]{3,0,1,2:T(2,128)(2,1)}), bf16[2,1,768,2048]{3,0,1,2:T(2,128)(2,1)}, u32[]{:S(2)}, u32[]{:S(2)}) async-start(bf16[2,1,768,2048]{3,0,1,2:T(2,128)(2,1)} %copy.50), calls=%async_computation.2 | async-start | bytes 12582912 | tf_op jit(solution)/shard_map/all_to_all | solution.py:84
  139.6 158.6 %all-to-all-start = ((bf16[2,64,12,2048]{3,0,2,1:T(2,128)(2,1)}), bf16[2,64,12,2048]{3,0,2,1:T(2,128)(2,1)}, u32[]{:S(2)}, u32[]{:S(2)}) async-start(bf16[2,64,12,2048]{3,0,2,1:T(2,128)(2,1)} %bitcast.73), calls=%async_computation | async-start | bytes 12582912 | tf_op jit(solution)/shard_map/all_to_all | solution.py:80
  160.0 151.5 %all-gather.3.cloned.1.call-start = ((), (), s32[]{:S(2)}) async-start(), calls=%async_computation.3 | async-start | bytes 5242880 | tf_op jit(solution)/shard_map/all_gather | solution.py:11
Sparse Core Ops, SparseCore 0:
  167.6 121.6 all-gather.2
where the time goes:
time: 340 us; the launch traced here: 333 us
  waiting for transfers between devices  183 us (54%)
  local copies, waits for them, and re-layouts  45.1 us (13%)
  matrix products  31.3 us (9%)
  starting transfers between devices  27.7 us (8%)
  other arithmetic  16.8 us (5%)
  blocking collectives  15.5 us (5%)
  between operations  14.2 us (4%)
    all_to_all x1, waiting for transfers between devices, shards(): lax.all_to_all(outgoing, 'dp', split_axis=1, concat_axis=2, tiled=True)  131 us
    all_to_all x1, waiting for transfers between devices, shards(): lax.all_to_all(back_rows[:, None], 'dp', split_axis=2, concat_axis=1, til...  52 us
    all_to_all x1, starting transfers between devices, shards(): lax.all_to_all(outgoing, 'dp', split_axis=1, concat_axis=2, tiled=True)  20.4 us
    convert_element_type x1, local copies, waits for them, and re-layouts, shards(): outgoing = jnp.einsum('mtj,mtd->mjd', dispatch_mat, features, preferred_e...  18.8 us
    broadcast_in_dim x1, local copies, waits for them, and re-layouts, shards(): back_rows[:, None]  18.8 us
    all_to_all x1, blocking collectives, shards(): lax.all_to_all(outgoing_gates, 'dp', split_axis=1, concat_axis=2, tiled=T...  15.5 us
    dot_general x1, matrix products, owner_work(): jnp.einsum('msd,msf->mdf', received_rows, scaled, preferred_element_type=...  13.3 us
    select_n x3, other arithmetic, lap(): return jnp.where(position < mine, longer, so_far)  7.74 us
  transfers between devices with their start and end apart: 3, of which 2 were waited for; matrix products, arithmetic and copies ran while one was open for 13% of the time, Pallas kernels for 0%

commit v1 on v0

v1 whole, which is shorter than its diff:
```python
import jax
import jax.numpy as jnp
from jax import lax
from jax.experimental import pallas as pl
from jax.experimental.pallas import tpu as pltpu
from jax.sharding import PartitionSpec as P

MESH = pl.DeviceIdType.MESH
M = 2
T = 64
D = 2048
F = 768
E = 64
CAP = 12
NB = 8
NI = 8
ROWS = NB * CAP
NC = 4
CW = D // NC
NT = (((1,), (1,)), ((), ()))
TN = (((0,), (0,)), ((), ()))
F32 = jnp.float32
BF16 = jnp.bfloat16


def dot(a, b, dims=(((1,), (0,)), ((), ()))):
    return lax.dot_general(a, b, dims, preferred_element_type=F32)


def iota(shape, dim):
    return lax.broadcasted_iota(jnp.int32, shape, dim)


def kernel(
    act, routes, gates, hcot, wgt, top,
    grad, fish, resid,
    meta, tok, hh, hht, gsend, gin, hc, wv, tv, scaled, bsend, bin_, rows,
    pown, psend, rin, ssend, sin, csend, cin, rstage, gstage, fstage,
    lsem, osem, mz_s, mz_r, tz_s, tz_r, mu_s, mu_r, tu_s, tu_r, g_s, g_r,
    r1_s, r1_r, r2_s, r2_r, r3_s, r3_r, d3_s, d3_r, ch_s, ch_r,
):
    sec = lax.axis_index("section")
    me = lax.axis_index("dp")
    y, x, z, c = me // 16, (me // 4) % 4, (me // 2) % 2, me % 2

    def index(yy, xx, zz, cc):
        return ((yy * 4 + xx) * 2 + zz) * 2 + cc

    def peer_u(m, du):
        if m == 0:
            return index((y + du) % 4, x, z, c)
        return index(y, (x + du) % 4, z, c)

    def peer_v(m, dv, dc):
        if m == 0:
            return index(y, (x + dv) % 4, z, (c + dc) % 2)
        return index((y + dv) % 4, x, z, (c + dc) % 2)

    peer_z = index(y, x, 1 - z, c)

    def remote(src, dst, ssem, rsem, dev):
        return pltpu.make_async_remote_copy(
            src_ref=src, dst_ref=dst, send_sem=ssem, recv_sem=rsem,
            device_id={"dp": dev}, device_id_type=MESH)

    act_cp = [pltpu.make_async_copy(act.at[m], tok.at[m, 0], lsem.at[m]) for m in range(M)]
    hc_cp = pltpu.make_async_copy(hcot, hc, lsem.at[2])
    w_cp = pltpu.make_async_copy(wgt, wv, lsem.at[3])
    t_cp = pltpu.make_async_copy(top, tv, lsem.at[4])
    for cp in act_cp + [hc_cp, w_cp, t_cp]:
        cp.start()

    bar = pltpu.get_barrier_semaphore()
    peers = [peer_z, index(y, x, z, 1 - c)]
    for m in range(M):
        for dv in range(1, 4):
            for dc in range(2):
                peers.append(peer_v(m, dv, dc))
    for p in peers:
        pl.semaphore_signal(bar, inc=1, device_id={"dp": p}, device_id_type=MESH)
    for ds in (1, 3):
        pl.semaphore_signal(bar, inc=1, device_id={"section": (sec + ds) % 4}, device_id_type=MESH)

    lane = iota((T, 128), 1)
    expert = lane & (E - 1)
    lower = (iota((T, T), 0) > iota((T, T), 1)).astype(F32).astype(BF16)
    for m in range(M):
        r = routes[m]
        g = gates[m].astype(F32)
        named = jnp.zeros((T, 128), F32)
        gate = jnp.zeros((T, 128), F32)
        for k in range(8):
            eq = r[:, k:k + 1] == expert
            named = jnp.where(eq, 1.0, named)
            gate = jnp.where(eq, g[:, k:k + 1], gate)
        pos = dot(lower, named.astype(BF16))
        meta[m, 0] = jnp.where(lane < E, jnp.where(named > 0.0, pos, 128.0), gate).astype(BF16)

    pl.semaphore_wait(bar, len(peers) + 2)

    mz = [remote(meta.at[m, 0], meta.at[m, 4], mz_s.at[m], mz_r.at[m], peer_z) for m in range(M)]
    tz = [remote(tok.at[m, 0], tok.at[m, 4], tz_s.at[m], tz_r.at[m], peer_z) for m in range(M)]
    mu = {}
    tu = {}
    for m in range(M):
        for zz in range(2):
            for du in range(1, 4):
                far = zz * 4 + (4 - du) % 4
                k = (m * 2 + zz) * 3 + du - 1
                mu[m, zz, du] = remote(meta.at[m, zz * 4], meta.at[m, far], mu_s.at[k], mu_r.at[k], peer_u(m, du))
                tu[m, zz, du] = remote(tok.at[m, zz * 4], tok.at[m, far], tu_s.at[k], tu_r.at[k], peer_u(m, du))
    for m in range(M):
        mz[m].start()
    for m in range(M):
        for du in range(1, 4):
            mu[m, 0, du].start()
    for m in range(M):
        act_cp[m].wait()
        tz[m].start()
        for du in range(1, 4):
            tu[m, 0, du].start()
    for m in range(M):
        mz[m].wait_recv()
        for du in range(1, 4):
            mu[m, 1, du].start()
    for m in range(M):
        for zz in range(2):
            for du in range(1, 4):
                mu[m, zz, du].wait_recv()

    def exchange_expert(m, i):
        dv, dc = i >> 1, i & 1
        if m == 0:
            return index(y, (x + dv) & 3, z, (c + dc) & 1)
        return index((y + dv) & 3, x, z, (c + dc) & 1)

    gcopy = {}
    for m in range(M):
        block = meta[m].reshape(NB * T, 128)
        l = iota((128, NI * ROWS), 1)
        i = (l * 683) >> 16
        sel = (iota((128, NI * ROWS), 0) == exchange_expert(m, i)).astype(F32).astype(BF16)
        l = iota((NB * T, NI * ROWS), 1)
        want = l - ((l * 683) >> 16) * ROWS - CAP * (iota((NB * T, NI * ROWS), 0) >> 6)
        hht[m] = (dot(block, sel) == want.astype(F32)).astype(F32).astype(BF16)
        r = iota((NI * ROWS, 128), 0)
        i = (r * 683) >> 16
        sel = (iota((NI * ROWS, 128), 1) == exchange_expert(m, i)).astype(F32).astype(BF16)
        r = iota((NI * ROWS, NB * T), 0)
        want = r - ((r * 683) >> 16) * ROWS - CAP * (iota((NI * ROWS, NB * T), 1) >> 6)
        hh[m] = (dot(sel, block, NT) == want.astype(F32)).astype(F32).astype(BF16)
        l = iota((128, NI * 128), 1)
        p = iota((128, NI * 128), 0)
        e = exchange_expert(m, l >> 7)
        sel = (p == e).astype(F32).astype(BF16)
        gsel = (p == e + E).astype(F32).astype(BF16)
        want = (iota((NB * T, NI * 128), 1) & 127) - CAP * (iota((NB * T, NI * 128), 0) >> 6)
        hit = dot(block, sel) == want.astype(F32)
        grow = jnp.sum(jnp.where(hit, dot(block, gsel), 0.0), axis=0, keepdims=True)
        for i in range(NI):
            row = jnp.broadcast_to(grow[:, i * 128:(i + 1) * 128], (16, 128)).astype(BF16)
            if i == 0:
                gin[m, 0] = row
                continue
            gsend[m, i] = row
            k = m * 7 + i - 1
            gcopy[m, i] = remote(gsend.at[m, i], gin.at[m, i], g_s.at[k], g_r.at[k], peer_v(m, i // 2, i % 2))
            gcopy[m, i].start()

    for m in range(M):
        tz[m].wait_recv()
        for du in range(1, 4):
            tu[m, 1, du].start()

    hc_cp.wait()
    for m in range(M):
        for i in range(1, NI):
            gcopy[m, i].wait_recv()
        for i in range(NI):
            dv, dc = i // 2, i % 2
            eye = iota((ROWS, 128), 0) == iota((ROWS, 128), 1)
            gcol = jnp.sum(jnp.where(eye, gin[m, i][0:1].astype(F32), 0.0), axis=1, keepdims=True)
            r = iota((ROWS, F), 0)
            b = (r * 171) >> 11
            q = r - b * CAP
            zs = (z + (b >> 2)) & 1
            us = b & 3
            if m == 0:
                j = index((y + us) & 3, (x + 4 - dv) % 4, zs, (c + dc) % 2)
            else:
                j = index((y + 4 - dv) % 4, (x + us) & 3, zs, (c + dc) % 2)
            pick = jnp.where(iota((ROWS, F), 1) == j * CAP + q, gcol, 0.0).astype(BF16)
            scaled[m, i * ROWS:(i + 1) * ROWS] = dot(pick, hc[m]).astype(BF16)

    w_cp.wait()
    r1 = {}
    d3 = {}
    for n in range(NC):
        for m in range(M):
            for i in range(1, NI):
                dv, dc = i // 2, i % 2
                k = (m * NC + n) * 7 + i - 1
                part = pl.ds(i * ROWS, ROWS)
                r1[m, n, i] = remote(bsend.at[m, n, part], bin_.at[m, n, part], r1_s.at[k], r1_r.at[k],
                                     peer_v(m, (4 - dv) % 4, dc))
                d3[m, n, i] = remote(bsend.at[m, n, part], rows.at[m, n, part], d3_s.at[k], d3_r.at[k],
                                     peer_v(m, dv, dc))
    for n in range(NC):
        for m in range(M):
            back = dot(scaled[m], wv[n * CW:(n + 1) * CW], NT).astype(BF16)
            bin_[m, n, 0:ROWS] = back[0:ROWS]
            bsend[m, n, ROWS:] = back[ROWS:]
            for i in range(1, NI):
                r1[m, n, i].start()

    for m in range(M):
        for zz in range(2):
            for du in range(1, 4):
                tu[m, zz, du].wait_recv()
    t_cp.wait()

    r2 = {}
    r3 = {}
    for n in range(NC):
        for m in range(M):
            k = m * NC + n
            r2[m, n] = remote(psend.at[m, n], rin.at[m, n], r2_s.at[k], r2_r.at[k], peer_z)
            for du in range(1, 4):
                k = (m * NC + n) * 3 + du - 1
                r3[m, n, du] = remote(ssend.at[m, n, du - 1], sin.at[m, n, du - 1], r3_s.at[k], r3_r.at[k],
                                      peer_u(m, du))
    ch = [pltpu.make_async_remote_copy(
        src_ref=csend.at[n], dst_ref=cin.at[n], send_sem=ch_s.at[n], recv_sem=ch_r.at[n],
        device_id={"section": (sec + 3) % 4}, device_id_type=MESH) for n in range(NC)]

    def combine(n):
        for m in range(M):
            for i in range(1, NI):
                r1[m, n, i].wait_recv()
            part = dot(hht[m], bin_[m, n])
            psend[m, n] = part[4 * T:].astype(BF16)
            r2[m, n].start()
            pown[m, n] = part[:4 * T]

    def send_rows(n):
        for m in range(M):
            for i in range(1, NI):
                r1[m, n, i].wait_send()
            gathered = tok[m, :, :, n * CW:(n + 1) * CW].reshape(NB * T, CW)
            out = dot(hh[m], gathered).astype(BF16)
            rows[m, n, 0:ROWS] = out[0:ROWS]
            bsend[m, n, ROWS:] = out[ROWS:]
            for i in range(1, NI):
                d3[m, n, i].start()

    def spread(n):
        for m in range(M):
            r2[m, n].wait_recv()
            total = pown[m, n] + rin[m, n].astype(F32)
            for du in range(1, 4):
                ssend[m, n, du - 1] = total[du * T:(du + 1) * T].astype(BF16)
                r3[m, n, du].start()
            pown[m, n, 0:T] = total[0:T]

    outs = {}

    def weights(n):
        slot = n % 2
        if n >= 2:
            for cp in outs[n - 2]:
                cp.wait()
        for m in range(M):
            for i in range(1, NI):
                d3[m, n, i].wait_recv()
        p0 = dot(rows[0, n], scaled[0], TN)
        p1 = dot(rows[1, n], scaled[1], TN)
        gstage[slot] = (p0 + p1).astype(BF16)
        fstage[slot] = (p0 * p0 + p1 * p1).astype(BF16)
        cut = pl.ds(n * CW, CW)
        outs[n] = [pltpu.make_async_copy(gstage.at[slot], grad.at[cut], osem.at[slot]),
                   pltpu.make_async_copy(fstage.at[slot], fish.at[cut], osem.at[2 + slot])]
        for cp in outs[n]:
            cp.start()

    @pl.when(sec == 3)
    def _():
        cin[...] = jnp.zeros_like(cin)

    def chain(n):
        for m in range(M):
            for du in range(1, 4):
                r3[m, n, du].wait_recv()

        @pl.when(sec < 3)
        def _():
            ch[n].wait_recv()

        for m in range(M):
            total = pown[m, n, 0:T] + cin[n, m].astype(F32)
            for du in range(1, 4):
                total = total + sin[m, n, du - 1].astype(F32)
            csend[n, m] = total.astype(BF16)
            cut = pl.ds(n * CW, CW)
            rstage[m, :, cut] = (tv[m, :, cut].astype(F32) + total).astype(BF16)

        @pl.when(sec > 0)
        def _():
            ch[n].start()

    for step in range(NC + 2):
        if step < NC:
            combine(step)
            send_rows(step)
        if 0 <= step - 1 < NC:
            spread(step - 1)
            weights(step - 1)
        if 0 <= step - 2 < NC:
            chain(step - 2)

    out_r = pltpu.make_async_copy(rstage, resid, lsem.at[5])
    out_r.start()
    for m in range(M):
        mz[m].wait_send()
        tz[m].wait_send()
        for i in range(1, NI):
            gcopy[m, i].wait_send()
        for zz in range(2):
            for du in range(1, 4):
                mu[m, zz, du].wait_send()
                tu[m, zz, du].wait_send()
        for n in range(NC):
            for i in range(1, NI):
                d3[m, n, i].wait_send()
            r2[m, n].wait_send()
            for du in range(1, 4):
                r3[m, n, du].wait_send()

    @pl.when(sec > 0)
    def _():
        for n in range(NC):
            ch[n].wait_send()

    for n in range(NC - 2, NC):
        for cp in outs[n]:
            cp.wait()
    out_r.wait()


def fused(act, routes, gates, hcot, wgt, top):
    hbm = pl.BlockSpec(memory_space=pl.ANY)
    vmem = pl.BlockSpec(memory_space=pltpu.VMEM)
    sem = pltpu.SemaphoreType.DMA
    v = pltpu.VMEM
    pairs = [M, M, M * 6, M * 6, M * 7, M * NC * 7, M * NC, M * NC * 3, M * NC * 7, NC]
    sems = [sem((6,)), sem((4,))]
    for n in pairs:
        sems += [sem((n,)), sem((n,))]
    return pl.pallas_call(
        kernel,
        out_shape=(
            jax.ShapeDtypeStruct((D, F), BF16),
            jax.ShapeDtypeStruct((D, F), BF16),
            jax.ShapeDtypeStruct((M, T, D), BF16),
        ),
        in_specs=[hbm, vmem, vmem, hbm, hbm, hbm],
        out_specs=(hbm, hbm, hbm),
        scratch_shapes=[
            v((M, NB, T, 128), BF16),
            v((M, NB, T, D), BF16),
            v((M, NI * ROWS, NB * T), BF16),
            v((M, NB * T, NI * ROWS), BF16),
            v((M, NI, 16, 128), BF16),
            v((M, NI, 16, 128), BF16),
            v((M, F, F), BF16),
            v((D, F), BF16),
            v((M, T, D), BF16),
            v((M, NI * ROWS, F), BF16),
            v((M, NC, NI * ROWS, CW), BF16),
            v((M, NC, NI * ROWS, CW), BF16),
            v((M, NC, NI * ROWS, CW), BF16),
            v((M, NC, 4 * T, CW), F32),
            v((M, NC, 4 * T, CW), BF16),
            v((M, NC, 4 * T, CW), BF16),
            v((M, NC, 3, T, CW), BF16),
            v((M, NC, 3, T, CW), BF16),
            v((NC, M, T, CW), BF16),
            v((NC, M, T, CW), BF16),
            v((M, T, D), BF16),
            v((2, CW, F), BF16),
            v((2, CW, F), BF16),
        ] + sems,
        compiler_params=pltpu.CompilerParams(
            collective_id=0, has_side_effects=True, vmem_limit_bytes=62 * 2**20),
        cost_estimate=pl.CostEstimate(flops=18 * 10**9, bytes_accessed=26 * 10**6, transcendentals=0),
        name="expert_backward",
    )(act, routes, gates, hcot, wgt, top)


def shards(activations, routes, gates, hidden_cot, weight, top_cot):
    grad, fish, resid = fused(
        activations[0], routes[0], gates[0], hidden_cot[0, :, 0], weight[0, 0], top_cot)
    return grad[None, None], fish[None, None], resid[None]


def solution(mesh):
    return jax.shard_map(
        shards,
        mesh=mesh,
        in_specs=(
            P("section", None, "dp", None),
            P("section", None, "dp", None),
            P("section", None, "dp", None),
            P("section", None, "dp", None, None),
            P("section", "dp", None, None),
            P(None, "dp", None),
        ),
        out_specs=(
            P("section", "dp", None, None),
            P("section", "dp", None, None),
            P("section", None, "dp", None),
        ),
        check_vma=False,
    )
```

time: 340 us -> 164 us (0.48); the launches traced: 333 us -> 164 us
  waiting for transfers between devices: 183 us -> 0 us
  Pallas kernels: 0 us -> 154 us
  local copies, waits for them, and re-layouts: 45.1 us -> 9.19 us
  matrix products: 31.3 us -> 0 us
  starting transfers between devices: 27.7 us -> 0 us
  other arithmetic: 16.8 us -> 0 us
  blocking collectives: 15.5 us -> 0 us
  between operations: 14.2 us -> 0.65 us
    all_to_all x2 -> x0, waiting for transfers between devices: 183 us -> none  [the longest x1 131 us: shards(): lax.all_to_all(outgoing, 'dp', split_axis=1, concat_axis=2, tiled=True)]
    pallas_call x0 -> x1, Pallas kernels: none -> 154 us  [fused(): pl.pallas_call(kernel, out_shape=(jax.ShapeDtypeStruct((D, F), BF16), jax...]
    dot_general x5 -> x0, matrix products: 31.3 us -> none  [the longest x1 13.3 us: owner_work(): jnp.einsum('msd,msf->mdf', received_rows, scaled, preferred_element_type=...]
    all_to_all x2 -> x0, starting transfers between devices: 27.7 us -> none  [the longest x1 20.4 us: shards(): lax.all_to_all(outgoing, 'dp', split_axis=1, concat_axis=2, tiled=True)]
    convert_element_type x3 -> x0, local copies, waits for them, and re-layouts: 19 us -> none  [the longest x1 18.8 us: shards(): outgoing = jnp.einsum('mtj,mtd->mjd', dispatch_mat, features, preferred_e...]
    broadcast_in_dim x1 -> x0, local copies, waits for them, and re-layouts: 18.8 us -> none  [shards(): back_rows[:, None]]
    all_to_all x1 -> x0, blocking collectives: 15.5 us -> none  [shards(): lax.all_to_all(outgoing_gates, 'dp', split_axis=1, concat_axis=2, tiled=T...]
    select_n x3 -> x0, other arithmetic: 7.74 us -> none  [lap(): return jnp.where(position < mine, longer, so_far)]
  transfers between devices with their start and end apart: 3 -> 0, of which waited for: 2 -> 0; matrix products, arithmetic and copies ran while one was open for 13% -> 0% of each run, Pallas kernels for 0% -> 0%
where the time goes in v1:
time: 164 us
  Pallas kernels  154 us (94%)
  local copies, waits for them, and re-layouts  9.19 us (6%)
    pallas_call x1, Pallas kernels, fused(): pl.pallas_call(kernel, out_shape=(jax.ShapeDtypeStruct((D, F), BF16), jax...  154 us
    unnamed x9, local copies, waits for them, and re-layouts  9.19 us

profile of v1, /device:TPU:6, one launch (start us, length us, event | category | flops | bytes accessed | tf_op | source)
XLA Modules:
  0.0 164.2 jit_solution(43621491545486489)
XLA Ops:
  0.6 1.4 copy.10
  2.0 1.4 copy.9
  3.4 154.4 %expert_backward.1 = (bf16[2048,768]{1,0:T(8,128)(2,1)}, bf16[2048,768]{1,0:T(8,128)(2,1)}, bf16[2,64,2048]{2,1,0:T(8,128)(2,1)}) custom-call(bf16[2,64,2048]{2,1,0:T(8,128)(2,1)} %bitcast.15, s32[2,64,8]{2,1,0:T(8,128)} %bitcast.11, bf16[2,64,8]{2,1,0:T(8,128)(2,1)} %bitcast.12, bf16[2,768,768]{2,1,0:T(8,128)(2,1)} %bitcast.14, bf16[2048,768]{1,0:T(8,128)(2,1)} %bitcast.13, ...), custom_call_target="tpu_custom_call" | custom-call | flops 17999998976 | bytes 26000000 | tf_op jit(solution)/shard_map/expert_backward/pallas_call | solution.py:358
  157.9 0.0 copy-start
  157.9 3.9 %copy.14 = bf16[1,1,2048,768]{3,2,1,0:T(8,128)(2,1)} copy(bf16[1,1,2048,768]{3,2,1,0:T(8,128)(2,1)} %bitcast.9) | data formatting | bytes 6291456
  161.8 0.0 copy-done
  161.8 0.0 copy-start.1
  161.8 1.7 %copy.15 = bf16[1,1,2048,768]{3,2,1,0:T(8,128)(2,1)} copy(bf16[1,1,2048,768]{3,2,1,0:T(8,128)(2,1)S(1)} %bitcast.8) | data formatting | bytes 6291456
  163.4 0.0 copy-done.1
  163.5 0.8 copy.16
Async XLA Ops:
  157.9 3.9 %copy-start = (bf16[2048,768]{1,0:T(8,128)(2,1)S(1)}, bf16[2048,768]{1,0:T(8,128)(2,1)}, u32[]{:S(2)}) copy-start(bf16[2048,768]{1,0:T(8,128)(2,1)} %get-tuple-element.7) | copy-start | bytes 9437188
  161.8 1.7 %copy-start.1 = (bf16[2,64,2048]{2,1,0:T(8,128)(2,1)S(1)}, bf16[2,64,2048]{2,1,0:T(8,128)(2,1)}, u32[]{:S(2)}) copy-start(bf16[2,64,2048]{2,1,0:T(8,128)(2,1)} %get-tuple-element.8) | copy-start | bytes 1572868

commit v2 on v1

v2 whole, which is shorter than its diff:
```python
import jax
import jax.numpy as jnp
from jax import lax
from jax.experimental import pallas as pl
from jax.experimental.pallas import tpu as pltpu
from jax.sharding import PartitionSpec as P

MESH = pl.DeviceIdType.MESH
M = 2
T = 64
D = 2048
F = 768
E = 64
CAP = 12
NB = 8
NI = 8
ROWS = NB * CAP
NC = 4
CW = D // NC
NT = (((1,), (1,)), ((), ()))
TN = (((0,), (0,)), ((), ()))
F32 = jnp.float32
BF16 = jnp.bfloat16


def dot(a, b, dims=(((1,), (0,)), ((), ()))):
    return lax.dot_general(a, b, dims, preferred_element_type=F32)


def iota(shape, dim):
    return lax.broadcasted_iota(jnp.int32, shape, dim)


class Copy:
    def __init__(self, copy, started):
        self.copy, self.started = copy, started
        self.sent = self.received = False

    def start(self):
        self.copy.start()
        self.started.append(self)

    def wait_recv(self):
        if not self.received:
            self.copy.wait_recv()
        self.received = True

    def wait_send(self):
        if not self.sent:
            self.copy.wait_send()
        self.sent = True


def kernel(
    act, routes, gates, hcot, wgt, top,
    grad, fish, resid,
    slot, meta, tok, hh, hht, gsend, gin, pick, hc, wv, tv, scaled, bsend, bin_, rows,
    pown, psend, rin, ssend, sin, lsend, lin, csend, cin, rstage, gstage, fstage,
    lsem, osem, tz_s, tz_r, su_s, su_r, mu_s, mu_r, tu_s, tu_r, tf_s, tf_r, g_s, g_r,
    r1_s, r1_r, r2_s, r2_r, r3_s, r3_r, d3_s, d3_r, ch_s, ch_r,
):
    sec = lax.axis_index("section")
    me = lax.axis_index("dp")
    y, x, z, c = me // 16, (me // 4) % 4, (me // 2) % 2, me % 2

    def index(yy, xx, zz, cc):
        return ((yy * 4 + xx) * 2 + zz) * 2 + cc

    def peer_u(m, du, dz=0):
        if m == 0:
            return index((y + du) % 4, x, (z + dz) % 2, c)
        return index(y, (x + du) % 4, (z + dz) % 2, c)

    def peer_v(m, dv, dc):
        if m == 0:
            return index(y, (x + dv) % 4, z, (c + dc) % 2)
        return index((y + dv) % 4, x, z, (c + dc) % 2)

    peer_z = index(y, x, 1 - z, c)

    started = []

    def remote(src, dst, ssem, rsem, dev):
        return Copy(pltpu.make_async_remote_copy(
            src_ref=src, dst_ref=dst, send_sem=ssem, recv_sem=rsem,
            device_id={"dp": dev}, device_id_type=MESH), started)

    act_cp = [pltpu.make_async_copy(act.at[m], tok.at[m, 0], lsem.at[m]) for m in range(M)]
    hc_cp = pltpu.make_async_copy(hcot, hc, lsem.at[2])
    w_cp = pltpu.make_async_copy(wgt, wv, lsem.at[3])
    t_cp = pltpu.make_async_copy(top, tv, lsem.at[4])
    for cp in act_cp + [hc_cp, w_cp, t_cp]:
        cp.start()

    bar = pltpu.get_barrier_semaphore()
    peers = [peer_z, index(y, x, z, 1 - c)]
    for du in range(1, 4):
        peers += [index((y + du) % 4, x, 1 - z, c), index(y, (x + du) % 4, 1 - z, c)]
    for m in range(M):
        for dv in range(1, 4):
            for dc in range(2):
                peers.append(peer_v(m, dv, dc))
    for p in peers:
        pl.semaphore_signal(bar, inc=1, device_id={"dp": p}, device_id_type=MESH)
    for ds in (1, 2, 3):
        pl.semaphore_signal(bar, inc=1, device_id={"section": (sec + ds) % 4}, device_id_type=MESH)

    expert = iota((128, T), 0) & (E - 1)
    lower = (iota((T, T), 0) > iota((T, T), 1)).astype(F32).astype(BF16)
    same = (iota((T, T), 0) == iota((T, T), 1)).astype(F32).astype(BF16)
    for m in range(M):
        r = routes[m]
        g = gates[m].astype(F32)
        named = jnp.zeros((128, T), F32)
        gate = jnp.zeros((128, T), F32)
        for k in range(8):
            eq = r[k:k + 1] == expert
            named = jnp.where(eq, 1.0, named)
            gate = jnp.where(eq, g[k:k + 1], gate)
        named = named.astype(BF16)
        pos = jnp.where(dot(same, named, NT) > 0.0, dot(lower, named, NT), 128.0)
        gate = dot(same, gate.astype(BF16), NT)
        meta[m, 0] = pos.astype(BF16)
        slots = [jnp.sum(jnp.where(pos == float(q), gate, 0.0), axis=0, keepdims=True) for q in range(CAP)]
        slots.append(jnp.zeros((16 - CAP, 128), F32))
        slot[m, 0] = jnp.concatenate(slots, axis=0).astype(BF16)

    pl.semaphore_wait(bar, len(peers) + 3)

    tz = [remote(tok.at[m, 0], tok.at[m, 4], tz_s.at[m], tz_r.at[m], peer_z) for m in range(M)]
    mu = {}
    su = {}
    tu = {}
    tf = {}
    for m in range(M):
        for zz in range(2):
            at = zz * 4
            for du in range(4):
                if zz or du:
                    k = m * 7 + zz * 4 + du - 1
                    su[m, zz, du] = remote(slot.at[m, 0], slot.at[m, at + (4 - du) % 4], su_s.at[k], su_r.at[k],
                                           peer_u(m, du, zz))
                    mu[m, zz, du] = remote(meta.at[m, 0], meta.at[m, at + (4 - du) % 4], mu_s.at[k], mu_r.at[k],
                                           peer_u(m, du, zz))
            for side, du in enumerate((1, 3)):
                k = (m * 2 + zz) * 2 + side
                half = pl.ds(side * (T // 2), T // 2)
                tu[m, zz, side] = remote(tok.at[m, at], tok.at[m, at + 4 - du], tu_s.at[k], tu_r.at[k], peer_u(m, du))
                tf[m, zz, side] = remote(tok.at[m, at + 4 - du, half], tok.at[m, at + 2, half],
                                         tf_s.at[k], tf_r.at[k], peer_u(m, du))

    def forward(zz):
        for m in range(M):
            for side in range(2):
                tu[m, zz, side].wait_recv()
                tf[m, zz, side].start()

    for at in su:
        su[at].start()
    for m in range(M):
        act_cp[m].wait()
        for side in range(2):
            tu[m, 0, side].start()
        tz[m].start()
    for at in su:
        su[at].wait_recv()

    def exchange_expert(m, i):
        dv, dc = i >> 1, i & 1
        if m == 0:
            return index(y, (x + dv) & 3, z, (c + dc) & 1)
        return index((y + dv) & 3, x, z, (c + dc) & 1)

    gcopy = {}
    for m in range(M):
        table = slot[m].reshape(NB * 16, 128)
        sel = (iota((16, 128), 1) == exchange_expert(m, iota((16, 128), 0) & 7)).astype(F32).astype(BF16)
        gsend[m] = dot(sel, table, NT).astype(BF16)
        for i in range(1, NI):
            k = m * 7 + i - 1
            gcopy[m, i] = remote(gsend.at[m], gin.at[m, i], g_s.at[k], g_r.at[k], peer_v(m, i // 2, i % 2))
            gcopy[m, i].start()

    def row_masks(m):
        block = meta[m].reshape(NB * T, 128)
        r = iota((NI * ROWS, 128), 0)
        i = (r * 683) >> 16
        sel = (iota((NI * ROWS, 128), 1) == exchange_expert(m, i)).astype(F32).astype(BF16)
        r = iota((NI * ROWS, NB * T), 0)
        want = r - ((r * 683) >> 16) * ROWS - CAP * (iota((NI * ROWS, NB * T), 1) >> 6)
        hh[m] = (dot(sel, block, NT) == want.astype(F32)).astype(F32).astype(BF16)

    for at in mu:
        mu[at].start()
    forward(0)
    for m in range(M):
        tz[m].wait_recv()
        for side in range(2):
            tu[m, 1, side].start()

    hc_cp.wait()
    r = iota((ROWS, 128), 0)
    b = (r * 171) >> 11
    place = (iota((ROWS, 128), 1) == b * 16 + r - b * CAP).astype(F32).astype(BF16)
    r = iota((ROWS, 1), 0)
    b = (r * 171) >> 11
    q = r - b * CAP
    zs = (z + (b >> 2)) & 1
    us = b & 3
    for m in range(M):
        for i in range(1, NI):
            gcopy[m, i].wait_recv()
        for i in range(NI):
            dv, dc = i // 2, i % 2
            got = gsend[m] if i == 0 else gin[m, i]
            gcol = dot(place, got, NT)[:, i:i + 1]
            if m == 0:
                j = index((y + us) & 3, (x + 4 - dv) % 4, zs, (c + dc) % 2)
            else:
                j = index((y + 4 - dv) % 4, (x + us) & 3, zs, (c + dc) % 2)
            pick[i * ROWS:(i + 1) * ROWS] = jnp.where(iota((ROWS, F), 1) == j * CAP + q, gcol, 0.0).astype(BF16)
        scaled[m] = dot(pick[...], hc[m]).astype(BF16)

    w_cp.wait()
    r1 = {}
    d3 = {}
    for n in range(NC):
        for m in range(M):
            for i in range(1, NI):
                dv, dc = i // 2, i % 2
                k = (m * NC + n) * 7 + i - 1
                part = pl.ds(i * ROWS, ROWS)
                r1[m, n, i] = remote(bsend.at[m, n, part], bin_.at[m, n, part], r1_s.at[k], r1_r.at[k],
                                     peer_v(m, (4 - dv) % 4, dc))
                d3[m, n, i] = remote(bsend.at[m, n, part], rows.at[m, n, part], d3_s.at[k], d3_r.at[k],
                                     peer_v(m, dv, dc))
    for n in range(NC):
        for m in range(M):
            back = dot(scaled[m], wv[n * CW:(n + 1) * CW], NT).astype(BF16)
            bin_[m, n, 0:ROWS] = back[0:ROWS]
            bsend[m, n, ROWS:] = back[ROWS:]
            for i in range(1, NI):
                r1[m, n, i].start()

    forward(1)
    for at in mu:
        mu[at].wait_recv()
    for m in range(M):
        block = meta[m].reshape(NB * T, 128)
        l = iota((128, NI * ROWS), 1)
        i = (l * 683) >> 16
        sel = (iota((128, NI * ROWS), 0) == exchange_expert(m, i)).astype(F32).astype(BF16)
        l = iota((NB * T, NI * ROWS), 1)
        want = l - ((l * 683) >> 16) * ROWS - CAP * (iota((NB * T, NI * ROWS), 0) >> 6)
        hht[m] = (dot(block, sel) == want.astype(F32)).astype(F32).astype(BF16)

    for m in range(M):
        row_masks(m)
    t_cp.wait()

    r2 = {}
    r3 = {}
    for m in range(M):
        n = NC - 1
        near = pl.ds(0, T)
        r2[m, n] = remote(psend.at[m, n, near], rin.at[m, n, near], r2_s.at[m * NC + n], r2_r.at[m * NC + n], peer_z)
        for du in range(1, 4):
            k = (m * NC + n) * 3 + du - 1
            r3[m, n, du] = remote(lsend.at[m, du - 1], lin.at[m, du - 1], r3_s.at[k], r3_r.at[k], peer_u(m, du))
    for n in range(NC - 1):
        for m in range(M):
            k = m * NC + n
            r2[m, n] = remote(psend.at[m, n], rin.at[m, n], r2_s.at[k], r2_r.at[k], peer_z)
            for du in range(1, 4):
                k = (m * NC + n) * 3 + du - 1
                r3[m, n, du] = remote(ssend.at[m, n, du - 1], sin.at[m, n, du - 1], r3_s.at[k], r3_r.at[k],
                                      peer_u(m, du))
    down = {(n, k, m): pltpu.make_async_remote_copy(
        src_ref=csend.at[n, m], dst_ref=cin.at[k - 1, n, m],
        send_sem=ch_s.at[(n * 3 + k - 1) * M + m], recv_sem=ch_r.at[(n * 3 + k - 1) * M + m],
        device_id={"section": (sec + 4 - k) % 4}, device_id_type=MESH)
        for n in range(NC) for k in range(1, 4) for m in range(M)}

    def combine(n):
        for m in range(M):
            for i in range(1, NI):
                r1[m, n, i].wait_recv()
            part = dot(hht[m], bin_[m, n])
            if n == NC - 1:
                for zz in range(2):
                    for du in range(4):
                        one = part[(zz * 4 + du) * T:(zz * 4 + du + 1) * T]
                        if du == 0:
                            pown[m, n, zz * T:(zz + 1) * T] = one
                        else:
                            lsend[m, du - 1, zz] = one.astype(BF16)
                for du in range(1, 4):
                    r3[m, n, du].start()
                continue
            psend[m, n] = part[4 * T:].astype(BF16)
            r2[m, n].start()
            pown[m, n] = part[:4 * T]

    def send_rows(n):
        for m in range(M):
            for i in range(1, NI):
                r1[m, n, i].wait_send()
            gathered = tok[m, :, :, n * CW:(n + 1) * CW].reshape(NB * T, CW)
            out = dot(hh[m], gathered).astype(BF16)
            rows[m, n, 0:ROWS] = out[0:ROWS]
            bsend[m, n, ROWS:] = out[ROWS:]
            for i in range(1, NI):
                d3[m, n, i].start()

    def spread(n):
        for m in range(M):
            if n == NC - 1:
                total = [pown[m, n, zz * T:(zz + 1) * T] for zz in range(2)]
                for du in range(1, 4):
                    r3[m, n, du].wait_recv()
                    total = [total[zz] + lin[m, du - 1, zz].astype(F32) for zz in range(2)]
                psend[m, n, 0:T] = total[1].astype(BF16)
                r2[m, n].start()
                pown[m, n, 0:T] = total[0]
                continue
            r2[m, n].wait_recv()
            total = pown[m, n] + rin[m, n].astype(F32)
            for du in range(1, 4):
                ssend[m, n, du - 1] = total[du * T:(du + 1) * T].astype(BF16)
                r3[m, n, du].start()
            pown[m, n, 0:T] = total[0:T]

    outs = {}

    def weights(n):
        turn = n % 2
        if n >= 2:
            for cp in outs[n - 2]:
                cp.wait()
        for m in range(M):
            for i in range(1, NI):
                d3[m, n, i].wait_recv()
        p0 = dot(rows[0, n], scaled[0], TN)
        p1 = dot(rows[1, n], scaled[1], TN)
        gstage[turn] = (p0 + p1).astype(BF16)
        fstage[turn] = (p0 * p0 + p1 * p1).astype(BF16)
        cut = pl.ds(n * CW, CW)
        outs[n] = [pltpu.make_async_copy(gstage.at[turn], grad.at[cut], osem.at[turn]),
                   pltpu.make_async_copy(fstage.at[turn], fish.at[cut], osem.at[2 + turn])]
        for cp in outs[n]:
            cp.start()

    for k in range(1, 4):
        @pl.when(sec > 3 - k)
        def _():
            cin[k - 1] = jnp.zeros_like(cin[k - 1])

    def terms(n):
        for m in range(M):
            if n == NC - 1:
                r2[m, n].wait_recv()
                total = pown[m, n, 0:T] + rin[m, n, 0:T].astype(F32)
            else:
                total = pown[m, n, 0:T]
                for du in range(1, 4):
                    r3[m, n, du].wait_recv()
                    total = total + sin[m, n, du - 1].astype(F32)
            csend[n, m] = total.astype(BF16)
            pown[m, n, 0:T] = total
            for k in range(1, 4):
                @pl.when(sec >= k)
                def _():
                    down[n, k, m].start()

    def sums(n):
        cut = pl.ds(n * CW, CW)
        for m in range(M):
            total = tv[m, :, cut].astype(F32) + pown[m, n, 0:T]
            for k in range(1, 4):
                @pl.when(sec <= 3 - k)
                def _():
                    down[n, k, m].wait_recv()
                total = total + cin[k - 1, n, m].astype(F32)
            rstage[m, :, cut] = total.astype(BF16)

    def gathered_all():
        for m in range(M):
            for zz in range(2):
                for side in range(2):
                    tf[m, zz, side].wait_recv()

    plan = [(combine, 0), (combine, 1), (spread, 0), (combine, 2), (gathered_all,), (send_rows, 0), (terms, 0),
            (spread, 1), (combine, 3), (send_rows, 1), (terms, 1), (spread, 2), (spread, 3), (send_rows, 2),
            (terms, 2), (send_rows, 3), (terms, 3), (weights, 0), (sums, 0), (weights, 1), (sums, 1), (weights, 2),
            (sums, 2), (sums, 3), (weights, 3)]
    for step, *at in plan:
        step(*at)

    out_r = pltpu.make_async_copy(rstage, resid, lsem.at[5])
    out_r.start()
    for cp in started:
        cp.wait_recv()
        cp.wait_send()

    for k in range(1, 4):
        @pl.when(sec >= k)
        def _():
            for n in range(NC):
                for m in range(M):
                    down[n, k, m].wait_send()

    for n in outs:
        if n + 2 not in outs:
            for cp in outs[n]:
                cp.wait()
    out_r.wait()


def fused(act, routes, gates, hcot, wgt, top):
    hbm = pl.BlockSpec(memory_space=pl.ANY)
    vmem = pl.BlockSpec(memory_space=pltpu.VMEM)
    sem = pltpu.SemaphoreType.DMA
    v = pltpu.VMEM
    pairs = [M, M * 7, M * 7, M * 4, M * 4, M * 7, M * NC * 7, M * NC, M * NC * 3, M * NC * 7, M * NC * 3]
    sems = [sem((6,)), sem((4,))]
    for n in pairs:
        sems += [sem((n,)), sem((n,))]
    return pl.pallas_call(
        kernel,
        out_shape=(
            jax.ShapeDtypeStruct((D, F), BF16),
            jax.ShapeDtypeStruct((D, F), BF16),
            jax.ShapeDtypeStruct((M, T, D), BF16),
        ),
        in_specs=[hbm, vmem, vmem, hbm, hbm, hbm],
        out_specs=(hbm, hbm, hbm),
        scratch_shapes=[
            v((M, NB, 16, 128), BF16),
            v((M, NB, T, 128), BF16),
            v((M, NB, T, D), BF16),
            v((M, NI * ROWS, NB * T), BF16),
            v((M, NB * T, NI * ROWS), BF16),
            v((M, 16, 128), BF16),
            v((M, NI, 16, 128), BF16),
            v((F, F), BF16),
            v((M, F, F), BF16),
            v((D, F), BF16),
            v((M, T, D), BF16),
            v((M, NI * ROWS, F), BF16),
            v((M, NC, NI * ROWS, CW), BF16),
            v((M, NC, NI * ROWS, CW), BF16),
            v((M, NC, NI * ROWS, CW), BF16),
            v((M, NC, 4 * T, CW), F32),
            v((M, NC, 4 * T, CW), BF16),
            v((M, NC, 4 * T, CW), BF16),
            v((M, NC - 1, 3, T, CW), BF16),
            v((M, NC - 1, 3, T, CW), BF16),
            v((M, 3, 2, T, CW), BF16),
            v((M, 3, 2, T, CW), BF16),
            v((NC, M, T, CW), BF16),
            v((3, NC, M, T, CW), BF16),
            v((M, T, D), BF16),
            v((2, CW, F), BF16),
            v((2, CW, F), BF16),
        ] + sems,
        compiler_params=pltpu.CompilerParams(
            collective_id=0, has_side_effects=True, vmem_limit_bytes=62 * 2**20),
        cost_estimate=pl.CostEstimate(flops=18 * 10**9, bytes_accessed=26 * 10**6, transcendentals=0),
        name="expert_backward",
    )(act, routes, gates, hcot, wgt, top)


def shards(activations, routes, gates, hidden_cot, weight, top_cot):
    grad, fish, resid = fused(
        activations[0], jnp.swapaxes(routes[0], 1, 2), jnp.swapaxes(gates[0], 1, 2), hidden_cot[0, :, 0], weight[0, 0], top_cot)
    return grad[None, None], fish[None, None], resid[None]


def solution(mesh):
    return jax.shard_map(
        shards,
        mesh=mesh,
        in_specs=(
            P("section", None, "dp", None),
            P("section", None, "dp", None),
            P("section", None, "dp", None),
            P("section", None, "dp", None, None),
            P("section", "dp", None, None),
            P(None, "dp", None),
        ),
        out_specs=(
            P("section", "dp", None, None),
            P("section", "dp", None, None),
            P("section", None, "dp", None),
        ),
        check_vma=False,
    )
```

time: 164 us -> 140 us (0.85)
  the two profiles are of different devices: /device:TPU:6 before, /device:TPU:33 now
where the time goes in v2:
time: 140 us
  Pallas kernels  133 us (95%)
  local copies, waits for them, and re-layouts  6.37 us (5%)
    pallas_call x1, Pallas kernels, fused(): pl.pallas_call(kernel, out_shape=(jax.ShapeDtypeStruct((D, F), BF16), jax...  133 us
    unnamed x7, local copies, waits for them, and re-layouts  6.37 us

profile of v2, /device:TPU:33, one launch (start us, length us, event | category | flops | bytes accessed | tf_op | source)
XLA Modules:
  0.0 140.3 jit_solution(909271278362826438)
XLA Ops:
  0.6 133.3 %expert_backward.1 = (bf16[2048,768]{1,0:T(8,128)(2,1)}, bf16[2048,768]{1,0:T(8,128)(2,1)}, bf16[2,64,2048]{2,1,0:T(8,128)(2,1)}) custom-call(bf16[2,64,2048]{2,1,0:T(8,128)(2,1)} %bitcast.17, s32[2,8,64]{2,1,0:T(8,128)} %bitcast.18, bf16[2,8,64]{2,1,0:T(8,128)(2,1)} %bitcast.19, bf16[2,768,768]{2,1,0:T(8,128)(2,1)} %bitcast.16, bf16[2048,768]{1,0:T(8,128)(2,1)} %bitcast.15, ...), custom_call_target="tpu_custom_call" | custom-call | flops 17999998976 | bytes 26000000 | tf_op jit(solution)/shard_map/expert_backward/pallas_call | solution.py:428
  133.9 0.0 copy-start
  134.0 3.9 %copy.12 = bf16[1,1,2048,768]{3,2,1,0:T(8,128)(2,1)} copy(bf16[1,1,2048,768]{3,2,1,0:T(8,128)(2,1)} %bitcast.13) | data formatting | bytes 6291456
  137.9 0.0 copy-done
  137.9 0.0 copy-start.1
  137.9 1.7 %copy.13 = bf16[1,1,2048,768]{3,2,1,0:T(8,128)(2,1)} copy(bf16[1,1,2048,768]{3,2,1,0:T(8,128)(2,1)S(1)} %bitcast.12) | data formatting | bytes 6291456
  139.5 0.0 copy-done.1
  139.5 0.8 copy.14
Async XLA Ops:
  133.9 3.9 %copy-start = (bf16[2048,768]{1,0:T(8,128)(2,1)S(1)}, bf16[2048,768]{1,0:T(8,128)(2,1)}, u32[]{:S(2)}) copy-start(bf16[2048,768]{1,0:T(8,128)(2,1)} %get-tuple-element.7) | copy-start | bytes 9437188
  137.9 1.7 %copy-start.1 = (bf16[2,64,2048]{2,1,0:T(8,128)(2,1)S(1)}, bf16[2,64,2048]{2,1,0:T(8,128)(2,1)}, u32[]{:S(2)}) copy-start(bf16[2,64,2048]{2,1,0:T(8,128)(2,1)} %get-tuple-element.8) | copy-start | bytes 1572868

commit v3 on v2

--- a/solution.py
+++ b/solution.py
@@ -55,9 +55,9 @@
     act, routes, gates, hcot, wgt, top,
     grad, fish, resid,
     slot, meta, tok, hh, hht, gsend, gin, pick, hc, wv, tv, scaled, bsend, bin_, rows,
-    pown, psend, rin, ssend, sin, lsend, lin, csend, cin, rstage, gstage, fstage,
+    pown, psend, rin, ssend, sin, lsend, lin, csend, cin, xin, rstage, gstage, fstage,
     lsem, osem, tz_s, tz_r, su_s, su_r, mu_s, mu_r, tu_s, tu_r, tf_s, tf_r, g_s, g_r,
-    r1_s, r1_r, r2_s, r2_r, r3_s, r3_r, d3_s, d3_r, ch_s, ch_r,
+    r1_s, r1_r, r2_s, r2_r, r3_s, r3_r, d3_s, d3_r, ch_s, ch_r, x_s, x_r,
 ):
     sec = lax.axis_index("section")
     me = lax.axis_index("dp")
@@ -275,11 +275,13 @@
                 k = (m * NC + n) * 3 + du - 1
                 r3[m, n, du] = remote(ssend.at[m, n, du - 1], sin.at[m, n, du - 1], r3_s.at[k], r3_r.at[k],
                                       peer_u(m, du))
-    down = {(n, k, m): pltpu.make_async_remote_copy(
-        src_ref=csend.at[n, m], dst_ref=cin.at[k - 1, n, m],
-        send_sem=ch_s.at[(n * 3 + k - 1) * M + m], recv_sem=ch_r.at[(n * 3 + k - 1) * M + m],
-        device_id={"section": (sec + 4 - k) % 4}, device_id_type=MESH)
-        for n in range(NC) for k in range(1, 4) for m in range(M)}
+    ch = {(n, m): pltpu.make_async_remote_copy(
+        src_ref=csend.at[n, m], dst_ref=cin.at[n, m], send_sem=ch_s.at[n * M + m], recv_sem=ch_r.at[n * M + m],
+        device_id={"section": (sec + 3) % 4}, device_id_type=MESH) for n in range(NC - 1) for m in range(M)}
+    last = {(k, m): pltpu.make_async_remote_copy(
+        src_ref=csend.at[NC - 1, m], dst_ref=xin.at[k - 1, m],
+        send_sem=x_s.at[(k - 1) * M + m], recv_sem=x_r.at[(k - 1) * M + m],
+        device_id={"section": (sec + 4 - k) % 4}, device_id_type=MESH) for k in range(1, 4) for m in range(M)}
 
     def combine(n):
         for m in range(M):
@@ -350,37 +352,64 @@
         for cp in outs[n]:
             cp.start()
 
+    @pl.when(sec == 3)
+    def _():
+        cin[...] = jnp.zeros_like(cin)
+
     for k in range(1, 4):
         @pl.when(sec > 3 - k)
         def _():
-            cin[k - 1] = jnp.zeros_like(cin[k - 1])
-
-    def terms(n):
-        for m in range(M):
-            if n == NC - 1:
-                r2[m, n].wait_recv()
-                total = pown[m, n, 0:T] + rin[m, n, 0:T].astype(F32)
-            else:
-                total = pown[m, n, 0:T]
-                for du in range(1, 4):
-                    r3[m, n, du].wait_recv()
-                    total = total + sin[m, n, du - 1].astype(F32)
+            xin[k - 1] = jnp.zeros_like(xin[k - 1])
+
+    def chain(n):
+        for m in range(M):
+            for du in range(1, 4):
+                r3[m, n, du].copy.wait_recv()
+                r3[m, n, du].received = True
+
+            @pl.when(sec < 3)
+            def _():
+                ch[n, m].wait_recv()
+
+            total = pown[m, n, 0:T] + cin[n, m].astype(F32)
+            for du in range(1, 4):
+                total = total + sin[m, n, du - 1].astype(F32)
+            csend[n, m] = total.astype(BF16)
+
+            @pl.when(sec > 0)
+            def _():
+                ch[n, m].start()
+
+            cut = pl.ds(n * CW, CW)
+            rstage[m, :, cut] = (tv[m, :, cut].astype(F32) + total).astype(BF16)
+
+    def chain_on(section, n):
+        @pl.when(sec == section)
+        def _():
+            chain(n)
+
+    def last_terms():
+        n = NC - 1
+        for m in range(M):
+            r2[m, n].wait_recv()
+            total = pown[m, n, 0:T] + rin[m, n, 0:T].astype(F32)
             csend[n, m] = total.astype(BF16)
             pown[m, n, 0:T] = total
             for k in range(1, 4):
                 @pl.when(sec >= k)
                 def _():
-                    down[n, k, m].start()
-
-    def sums(n):
+                    last[k, m].start()
+
+    def last_sums():
+        n = NC - 1
         cut = pl.ds(n * CW, CW)
         for m in range(M):
             total = tv[m, :, cut].astype(F32) + pown[m, n, 0:T]
             for k in range(1, 4):
                 @pl.when(sec <= 3 - k)
                 def _():
-                    down[n, k, m].wait_recv()
-                total = total + cin[k - 1, n, m].astype(F32)
+                    last[k, m].wait_recv()
+                total = total + xin[k - 1, m].astype(F32)
             rstage[m, :, cut] = total.astype(BF16)
 
     def gathered_all():
@@ -389,10 +418,11 @@
                 for side in range(2):
                     tf[m, zz, side].wait_recv()
 
-    plan = [(combine, 0), (combine, 1), (spread, 0), (combine, 2), (gathered_all,), (send_rows, 0), (terms, 0),
-            (spread, 1), (combine, 3), (send_rows, 1), (terms, 1), (spread, 2), (spread, 3), (send_rows, 2),
-            (terms, 2), (send_rows, 3), (terms, 3), (weights, 0), (sums, 0), (weights, 1), (sums, 1), (weights, 2),
-            (sums, 2), (sums, 3), (weights, 3)]
+    plan = [(combine, 0), (combine, 1), (spread, 0), (combine, 2), (gathered_all,), (send_rows, 0), (chain_on, 3, 0),
+            (spread, 1), (combine, 3), (send_rows, 1), (chain_on, 3, 1), (chain_on, 2, 0), (spread, 2), (spread, 3),
+            (send_rows, 2), (chain_on, 3, 2), (chain_on, 2, 1), (chain_on, 1, 0), (send_rows, 3), (last_terms,),
+            (chain_on, 0, 0), (chain_on, 1, 1), (chain_on, 2, 2), (weights, 0), (chain_on, 0, 1), (weights, 1),
+            (chain_on, 1, 2), (weights, 2), (chain_on, 0, 2), (last_sums,), (weights, 3)]
     for step, *at in plan:
         step(*at)
 
@@ -402,12 +432,16 @@
         cp.wait_recv()
         cp.wait_send()
 
+    @pl.when(sec > 0)
+    def _():
+        for at in ch:
+            ch[at].wait_send()
+
     for k in range(1, 4):
         @pl.when(sec >= k)
         def _():
-            for n in range(NC):
-                for m in range(M):
-                    down[n, k, m].wait_send()
+            for m in range(M):
+                last[k, m].wait_send()
 
     for n in outs:
         if n + 2 not in outs:
@@ -421,7 +455,7 @@
     vmem = pl.BlockSpec(memory_space=pltpu.VMEM)
     sem = pltpu.SemaphoreType.DMA
     v = pltpu.VMEM
-    pairs = [M, M * 7, M * 7, M * 4, M * 4, M * 7, M * NC * 7, M * NC, M * NC * 3, M * NC * 7, M * NC * 3]
+    pairs = [M, M * 7, M * 7, M * 4, M * 4, M * 7, M * NC * 7, M * NC, M * NC * 3, M * NC * 7, M * (NC - 1), M * 3]
     sems = [sem((6,)), sem((4,))]
     for n in pairs:
         sems += [sem((n,)), sem((n,))]
@@ -458,7 +492,8 @@
             v((M, 3, 2, T, CW), BF16),
             v((M, 3, 2, T, CW), BF16),
             v((NC, M, T, CW), BF16),
-            v((3, NC, M, T, CW), BF16),
+            v((NC - 1, M, T, CW), BF16),
+            v((3, M, T, CW), BF16),
             v((M, T, D), BF16),
             v((2, CW, F), BF16),
             v((2, CW, F), BF16),
@@ -470,9 +505,42 @@
     )(act, routes, gates, hcot, wgt, top)
 
 
+def hand_on(grad, fish, resid, grad_out, fish_out, resid_out, gbuf, fbuf, rbuf, in_sems, out_sems):
+    cuts = [pl.ds(n * CW, CW) for n in range(NC)]
+    ways = []
+    for cut in cuts:
+        ways.append((grad.at[cut], gbuf.at[cut], grad_out.at[cut]))
+        ways.append((fish.at[cut], fbuf.at[cut], fish_out.at[cut]))
+    ways.append((resid, rbuf, resid_out))
+    loads = [pltpu.make_async_copy(a, b, in_sems.at[k]) for k, (a, b, _) in enumerate(ways)]
+    stores = [pltpu.make_async_copy(b, c, out_sems.at[k]) for k, (_, b, c) in enumerate(ways)]
+    for cp in loads:
+        cp.start()
+    for load, store in zip(loads, stores):
+        load.wait()
+        store.start()
+    for cp in stores:
+        cp.wait()
+
+
+def handed_on(*arrays):
+    hbm = pl.BlockSpec(memory_space=pl.ANY)
+    return pl.pallas_call(
+        hand_on,
+        out_shape=tuple(jax.ShapeDtypeStruct(a.shape, a.dtype) for a in arrays),
+        in_specs=[hbm] * 3,
+        out_specs=(hbm,) * 3,
+        scratch_shapes=[pltpu.VMEM(a.shape, a.dtype) for a in arrays]
+        + [pltpu.SemaphoreType.DMA((2 * NC + 1,))] * 2,
+        compiler_params=pltpu.CompilerParams(vmem_limit_bytes=60 * 2**20),
+        name="results",
+    )(*arrays)
+
+
 def shards(activations, routes, gates, hidden_cot, weight, top_cot):
     grad, fish, resid = fused(
         activations[0], jnp.swapaxes(routes[0], 1, 2), jnp.swapaxes(gates[0], 1, 2), hidden_cot[0, :, 0], weight[0, 0], top_cot)
+    grad, fish, resid = handed_on(grad, fish, resid)
     return grad[None, None], fish[None, None], resid[None]
 
 

time: 140 us -> 134 us (0.957)
  the two profiles are of different devices: /device:TPU:33 before, /device:TPU:6 now
where the time goes in v3:
time: 134 us; the launch traced here: 132 us
  Pallas kernels  132 us (99%)
    pallas_call x1, Pallas kernels, fused(): pl.pallas_call(kernel, out_shape=(jax.ShapeDtypeStruct((D, F), BF16), jax...  126 us
    pallas_call x1, Pallas kernels, handed_on(): pl.pallas_call(hand_on, out_shape=tuple((jax.ShapeDtypeStruct(a.shape, a....  5.68 us

profile of v3, /device:TPU:6, one launch (start us, length us, event | category | flops | bytes accessed | tf_op | source)
XLA Modules:
  0.0 132.5 jit_solution(1937468573327345825)
XLA Ops:
  0.6 126.0 %expert_backward.1 = (bf16[2048,768]{1,0:T(8,128)(2,1)}, bf16[2048,768]{1,0:T(8,128)(2,1)}, bf16[2,64,2048]{2,1,0:T(8,128)(2,1)}) custom-call(bf16[2,64,2048]{2,1,0:T(8,128)(2,1)} %bitcast.16, s32[2,8,64]{2,1,0:T(8,128)} %bitcast.18, bf16[2,8,64]{2,1,0:T(8,128)(2,1)} %bitcast.19, bf16[2,768,768]{2,1,0:T(8,128)(2,1)} %bitcast.15, bf16[2048,768]{1,0:T(8,128)(2,1)} %bitcast.12, ...), custom_call_target="tpu_custom_call" | custom-call | flops 17999998976 | bytes 26000000 | tf_op jit(solution)/shard_map/expert_backward/pallas_call | solution.py:462
  126.6 5.7 %results.1 = (bf16[2048,768]{1,0:T(8,128)(2,1)}, bf16[2048,768]{1,0:T(8,128)(2,1)}, bf16[2,64,2048]{2,1,0:T(8,128)(2,1)}) custom-call(bf16[2048,768]{1,0:T(8,128)(2,1)} %get-tuple-element.9.grad, bf16[2048,768]{1,0:T(8,128)(2,1)} %get-tuple-element.10.fish, bf16[2,64,2048]{2,1,0:T(8,128)(2,1)} %get-tuple-element.11.resid), custom_call_target="tpu_custom_call" | custom-call | tf_op jit(solution)/shard_map/results/pallas_call | solution.py:528

commit v4 on v3

--- a/solution.py
+++ b/solution.py
@@ -193,10 +193,6 @@
     for at in mu:
         mu[at].start()
     forward(0)
-    for m in range(M):
-        tz[m].wait_recv()
-        for side in range(2):
-            tu[m, 1, side].start()
 
     hc_cp.wait()
     r = iota((ROWS, 128), 0)
@@ -220,6 +216,11 @@
                 j = index((y + 4 - dv) % 4, (x + us) & 3, zs, (c + dc) % 2)
             pick[i * ROWS:(i + 1) * ROWS] = jnp.where(iota((ROWS, F), 1) == j * CAP + q, gcol, 0.0).astype(BF16)
         scaled[m] = dot(pick[...], hc[m]).astype(BF16)
+
+    for m in range(M):
+        tz[m].wait_recv()
+        for side in range(2):
+            tu[m, 1, side].start()
 
     w_cp.wait()
     r1 = {}

time: 134 us -> 133 us (level); the launches traced: 132 us -> 133 us
  no operation moved by 1% of the time
where the time goes in v4:
time: 133 us
  Pallas kernels  132 us (99%)
    pallas_call x1, Pallas kernels, fused(): pl.pallas_call(kernel, out_shape=(jax.ShapeDtypeStruct((D, F), BF16), jax...  127 us
    pallas_call x1, Pallas kernels, handed_on(): pl.pallas_call(hand_on, out_shape=tuple((jax.ShapeDtypeStruct(a.shape, a....  5.68 us

profile of v4, /device:TPU:6, one launch (start us, length us, event | category | flops | bytes accessed | tf_op | source)
XLA Modules:
  0.0 133.2 jit_solution(8312645307715341617)
XLA Ops:
  0.6 126.7 %expert_backward.1 = (bf16[2048,768]{1,0:T(8,128)(2,1)}, bf16[2048,768]{1,0:T(8,128)(2,1)}, bf16[2,64,2048]{2,1,0:T(8,128)(2,1)}) custom-call(bf16[2,64,2048]{2,1,0:T(8,128)(2,1)} %bitcast.16, s32[2,8,64]{2,1,0:T(8,128)} %bitcast.18, bf16[2,8,64]{2,1,0:T(8,128)(2,1)} %bitcast.19, bf16[2,768,768]{2,1,0:T(8,128)(2,1)} %bitcast.15, bf16[2048,768]{1,0:T(8,128)(2,1)} %bitcast.12, ...), custom_call_target="tpu_custom_call" | custom-call | flops 17999998976 | bytes 26000000 | tf_op jit(solution)/shard_map/expert_backward/pallas_call | solution.py:463
  127.4 5.7 %results.1 = (bf16[2048,768]{1,0:T(8,128)(2,1)}, bf16[2048,768]{1,0:T(8,128)(2,1)}, bf16[2,64,2048]{2,1,0:T(8,128)(2,1)}) custom-call(bf16[2048,768]{1,0:T(8,128)(2,1)} %get-tuple-element.9.grad, bf16[2048,768]{1,0:T(8,128)(2,1)} %get-tuple-element.10.fish, bf16[2,64,2048]{2,1,0:T(8,128)(2,1)} %get-tuple-element.11.resid), custom_call_target="tpu_custom_call" | custom-call | tf_op jit(solution)/shard_map/results/pallas_call | solution.py:529
